TPU v7x, 32 devices: a whole 2x2x4 slice. The times are simulated.
32 devices in a mesh: row: 8 (over y, x, core), col: 4 (over z).
Axes of the slice: x: 2, y: 2, z: 4, core: 2. Of those that a mesh axis runs over, the one named last changes fastest.
Arguments:
- slab_embed: float32 [16384, 768], P(('col', 'row')), may hold values from -1 to 1
- coverage_old: float32 [16384], P('col'), may hold values from 2 to 4.5
- sel_index: int32 [1024], P('row'), may hold values from 0 to 16383
- cand_index: int32 [1536], P('row'), may hold values from 0 to 16383
Outputs:
- coverage: float32 [16384], P('col')
- total_gain: float32 [1536], P('row')
Inputs may be any that keep to these rules, and one draw needn't show every extreme that they name: `sel_index`: indices into the slab. `cand_index`: indices into the slab.
All inputs are finite; a program needn't handle non-finite values.
Results may differ from a plain program's by a relative error of at most 0.00014.
Values sent between devices are 32-bit elements; how exact they have to be, the bound alone decides.
A program may use at most 128 MiB of HBM per device.

v0:
```python
import jax
import jax.numpy as jnp
from jax import lax
from jax.sharding import PartitionSpec as P


def similar(left, right):
    return lax.dot_general(
        left,
        right,
        (((1,), (1,)), ((), ())),
        precision=lax.Precision.HIGHEST,
        preferred_element_type=jnp.float32,
    )


def lookup(source, indices, first_row):
    position = indices - first_row
    inside = (position >= 0) & (position < source.shape[0])
    picked = jnp.take(source, jnp.clip(position, 0, source.shape[0] - 1), axis=0)
    return jnp.where(inside[:, None], picked, 0.0)


def body(slab_embed, coverage_old, sel_index, cand_index):
    col_id = lax.axis_index("col")
    gathered = lax.all_gather(slab_embed, "row", axis=0, tiled=True)
    first_row = col_id * gathered.shape[0]
    selected, chosen = lax.psum(
        (lookup(gathered, sel_index, first_row), lookup(gathered, cand_index, first_row)), "col"
    )
    partial_value = jnp.max(similar(selected, gathered), axis=0)
    reached = lax.pmax(partial_value, "row")
    coverage = jnp.maximum(coverage_old, reached)
    gain_part = jnp.sum(jnp.maximum(similar(chosen, gathered) - coverage[None, :], 0.0), axis=1)
    total_gain = lax.psum(gain_part, "col")
    return (coverage, total_gain)


def solution(mesh):
    in_specs = (P(("col", "row"), None), P("col"), P("row"), P("row"))
    out_specs = (P("col"), P("row"))
    return jax.shard_map(body, mesh=mesh, in_specs=in_specs, out_specs=out_specs, check_vma=False)
```

profile of v0, /device:TPU:0, one launch (start us, length us, event | category | flops | bytes accessed | tf_op | source)
XLA Modules:
  0.0 221.6 jit_solution(9260024606361572024)
XLA Ops:
  7.2 0.0 all-gather.2.cloned.1.call-start
  7.2 0.7 all-gather.2.cloned.1.call-update
  7.9 0.0 copy-start.2
  7.9 0.0 all-reduce.3.cloned.1.call-start
  8.0 0.7 compare_and_fusion
  8.7 0.7 compare_and_fusion.2
  9.3 75.4 %all-gather.2.cloned.1.call-done = f32[4096,768]{1,0:T(8,128)} async-done(((f32[512,768]{1,0:T(8,128)}), f32[4096,768]{1,0:T(8,128)}) %all-gather.2.cloned.1.call-update) | async-done | bytes 12582928 | tf_op jit(solution)/shard_map/all_gather | solution.py:26
  84.7 5.5 %gather_fusion = f32[128,768]{1,0:T(8,128)S(1)} fusion(f32[4096,768]{1,0:T(8,128)} %all-gather.2.cloned.1.call-done, s32[1024]{0:T(1024)S(1)} %pad_clamp_fusion.1), kind=kCustom, calls=%fused_computation | custom fusion | bytes 786944 | tf_op jit(solution)/shard_map/jit(_take)/gather | solution.py:20
  90.3 0.9 select_select_fusion.1
  91.2 5.8 %gather_fusion.1 = f32[192,768]{1,0:T(8,128)S(1)} fusion(f32[4096,768]{1,0:T(8,128)} %all-gather.2.cloned.1.call-done, s32[1024]{0:T(1024)S(1)} %pad_clamp_fusion), kind=kCustom, calls=%fused_computation.1 | custom fusion | bytes 1180416 | tf_op jit(solution)/shard_map/jit(_take)/gather | solution.py:20
  96.9 1.0 select_select_fusion
  97.9 0.0 all-reduce.3.cloned.1.call-update
  97.9 50.3 %all-reduce.3.cloned.1.call-done = (f32[128,768]{1,0:T(8,128)}, f32[192,768]{1,0:T(8,128)}) async-done(((f32[128,768]{1,0:T(8,128)}, f32[192,768]{1,0:T(8,128)}), (f32[128,768]{1,0:T(8,128)}, f32[192,768]{1,0:T(8,128)})) %all-reduce.3.cloned.1.call-update) | async-done | bytes 983056 | tf_op jit(solution)/shard_map/psum | solution.py:28
  148.2 0.0 copy-start
  148.2 15.8 %convolution_reduce_fusion = f32[4096]{0:T(1024)S(1)} fusion(f32[128,768]{1,0:T(8,128)} %get-tuple-element.2, f32[4096,768]{1,0:T(8,128)} %all-gather.2.cloned.1.call-done), kind=kOutput, calls=%fused_computation.5 | convolution fusion | flops 4832358400 | bytes 12992512 | tf_op jit(solution)/shard_map/dot_general | solution.py:8
  164.1 24.2 %pmax.7 = f32[4096]{0:T(1024)S(1)} all-reduce(f32[4096]{0:T(1024)S(1)} %convolution_reduce_fusion), channel_id=1, replica_groups=mesh['row'=8,'col'=4] {'row'}, use_global_device_ids=true, to_apply=%region_2.3 | all-reduce | flops 4096 | bytes 32768 | tf_op jit(solution)/shard_map/pmax | solution.py:32
  188.3 0.0 copy-done.2
  188.3 0.0 copy-start.1
  188.3 0.0 copy-done
  188.3 15.9 %fusion.1 = f32[192]{0:T(256)S(1)} fusion(f32[4096]{0:T(1024)S(1)} %max.19, f32[192,768]{1,0:T(8,128)S(1)} %copy-done, f32[4096,768]{1,0:T(8,128)} %all-gather.2.cloned.1.call-done), kind=kOutput, calls=%fused_computation.4 | convolution fusion | flops 7250116608 | bytes 13189888 | tf_op jit(solution)/shard_map/dot_general | solution.py:8
  204.2 10.6 %psum.23 = f32[192]{0:T(256)} all-reduce(f32[192]{0:T(256)S(1)} %fusion.1), channel_id=1, replica_groups=mesh['row'=8,'col'=4] {'col'}, use_global_device_ids=true, to_apply=%region_5.6 | all-reduce | flops 192 | bytes 1536 | tf_op jit(solution)/shard_map/psum | solution.py:35
  214.8 0.0 copy-done.1
  (3 shorter events, 0.0 us)
Async XLA Ops:
  7.2 77.6 %all-gather.2.cloned.1.call-start = ((), (), s32[]{:S(2)}) async-start(), calls=%async_computation | async-start | bytes 14155776 | tf_op jit(solution)/shard_map/all_gather | solution.py:26
  7.9 180.4 %copy-start.2 = (f32[4096]{0:T(1024)S(1)}, f32[4096]{0:T(1024)}, u32[]{:S(2)}) copy-start(f32[4096]{0:T(1024)} %param.5) | copy-start | bytes 49156
  7.9 140.3 %all-reduce.3.cloned.1.call-start = ((), (), s32[]{:S(2)}) async-start(), calls=%async_computation.1 | async-start | bytes 1966080 | tf_op jit(solution)/shard_map/psum | solution.py:28
  148.2 40.1 %copy-start = (f32[192,768]{1,0:T(8,128)S(1)}, f32[192,768]{1,0:T(8,128)}, u32[]{:S(2)}) copy-start(f32[192,768]{1,0:T(8,128)} %get-tuple-element.3) | copy-start | bytes 1769476
  188.3 26.5 %copy-start.1 = (f32[4096]{0:T(1024)}, f32[4096]{0:T(1024)S(1)}, u32[]{:S(2)}) copy-start(f32[4096]{0:T(1024)S(1)} %max.19) | copy-start | bytes 49156
Sparse Core Ops, SparseCore 0:
  9.9 74.8 all-gather.1
  98.1 50.1 all-reduce.2
where the time goes:
time: 222 us
  waiting for transfers between devices  126 us (57%)
  blocking collectives  34.8 us (16%)
  matrix products  31.7 us (14%)
  between operations  14.1 us (6%)
  local copies, waits for them, and re-layouts  11.3 us (5%)
  other arithmetic  3.22 us (1%)
    all_gather x1, waiting for transfers between devices, body(): gathered = lax.all_gather(slab_embed, 'row', axis=0, tiled=True)  75.4 us
    psum x1, waiting for transfers between devices, body(): lax.psum((lookup(gathered, sel_index, first_row), lookup(gathered, cand_i...  50.3 us
    dot_general x2, matrix products, similar(): lax.dot_general(left, right, (((1,), (1,)), ((), ())), precision=lax.Prec...  31.7 us
    pmax x1, blocking collectives, body(): reached = lax.pmax(partial_value, 'row')  24.2 us
    gather x2, local copies, waits for them, and re-layouts, lookup(): jnp.take(source, jnp.clip(position, 0, source.shape[0] - 1), axis=0)  11.3 us
    psum x1, blocking collectives, body(): total_gain = lax.psum(gain_part, 'col')  10.6 us
  transfers between devices with their start and end apart: 2, of which 2 were waited for; matrix products, arithmetic and copies ran while one was open for 1% of the time, Pallas kernels for 0%

commit v1 on v0

v1 whole, which is shorter than its diff:
```python
import functools

import jax
import jax.numpy as jnp
from jax import lax
from jax.experimental import pallas as pl
from jax.experimental.pallas import tpu as pltpu
from jax.sharding import PartitionSpec as P

MESH = pl.DeviceIdType.MESH
QUAD = 4
NT = (((1,), (1,)), ((), ()))


def similar(left, right):
    return lax.dot_general(
        left,
        right,
        (((1,), (1,)), ((), ())),
        precision=lax.Precision.HIGHEST,
        preferred_element_type=jnp.float32,
    )


def lookup(source, indices, first_row):
    position = indices - first_row
    inside = (position >= 0) & (position < source.shape[0])
    picked = jnp.take(source, jnp.clip(position, 0, source.shape[0] - 1), axis=0)
    return jnp.where(inside[:, None], picked, 0.0)


def any_draw(slab_embed, coverage_old, sel_index, cand_index):
    col_id = lax.axis_index("col")
    gathered = lax.all_gather(slab_embed, "row", axis=0, tiled=True)
    first_row = col_id * gathered.shape[0]
    selected, chosen = lax.psum(
        (lookup(gathered, sel_index, first_row), lookup(gathered, cand_index, first_row)), "col"
    )
    partial_value = jnp.max(similar(selected, gathered), axis=0)
    reached = lax.pmax(partial_value, "row")
    coverage = jnp.maximum(coverage_old, reached)
    gain_part = jnp.sum(jnp.maximum(similar(chosen, gathered) - coverage[None, :], 0.0), axis=1)
    return coverage, lax.psum(gain_part, "col")


def halves(value):
    high = value.astype(jnp.bfloat16)
    return high, (value - high.astype(jnp.float32)).astype(jnp.bfloat16)


def dot_nt(left, right):
    return lax.dot_general(left, right, NT, preferred_element_type=jnp.float32)


def kernel(
    R, C, cap, slab, cov_old, sel, cand, cand_col,
    cov_out, gain_out, flag_out,
    pts, ph, plo, qs, qh, ql, sc, idx, mx, cov, gp, gr,
    idx_send, idx_recv, core_send, core_recv, x_send, x_recv, f_send, f_recv,
    q_recv, ql_send, qr_send, qa_send, m_send, m_recv, c_send, c_recv, g_send, g_recv,
):
    A = R // QUAD
    NB = A * C
    ND = R * C
    rows = slab.shape[0]
    ns, nk = sel.shape[1], cand.shape[1]
    shift = rows.bit_length() - 1
    span = QUAD * rows
    r = lax.axis_index("row")
    c = lax.axis_index("col")
    me = c * R + r
    a = r // QUAD
    m = r % QUAD
    x, h = m // 2, m % 2
    m_core = 2 * x + (1 - h)
    m_x = 2 * (1 - x) + h
    m_diag = 2 * (1 - x) + (1 - h)
    base = a * QUAD
    chunk = rows // C

    def remote(src, dst, ssem, rsem, row, col):
        return pltpu.make_async_remote_copy(
            src_ref=src, dst_ref=dst, send_sem=ssem, recv_sem=rsem,
            device_id=(row, col), device_id_type=MESH,
        )

    barrier = pltpu.get_barrier_semaphore()

    def greet(i, carry):
        dev = (me + i) % ND
        pl.semaphore_signal(barrier, inc=1, device_id=(dev % R, dev // R), device_id_type=MESH)
        return carry

    lax.fori_loop(1, ND, greet, 0)
    idx[r, :, 0:ns] = sel[...]
    idx[r, :, ns : ns + nk] = cand[...]
    pl.semaphore_wait(barrier, ND - 1)

    def idx_copy(slot, to):
        return remote(idx.at[slot], idx.at[slot], idx_send.at[to], idx_recv.at[slot], to, c)

    for i in range(1, R):
        idx_copy(r, (r + i) % R).start()

    core_copy = remote(slab, pts.at[m], core_send.at[0], core_recv.at[0], base + m_core, c)
    core_copy.start()

    def x_copy(s):
        part = pl.ds(s * chunk, chunk)
        return remote(slab.at[part], pts.at[m, part], x_send.at[s], x_recv.at[s], base + m_x, c)

    def x_landed(s):
        part = pl.ds(s * chunk, chunk)
        return remote(slab.at[part], pts.at[m_x, part], x_send.at[s], x_recv.at[s], base + m_x, c)

    def f_copy(s):
        part = pl.ds(s * chunk, chunk)
        return remote(pts.at[m_x, part], pts.at[m_x, part], f_send.at[s], f_recv.at[s], base + m_core, c)

    def f_landed(s):
        part = pl.ds(s * chunk, chunk)
        return remote(pts.at[m_diag, part], pts.at[m_diag, part], f_send.at[s], f_recv.at[s], base + m_core, c)

    for s in range(C):
        x_copy(s).start()

    def split_points(source, slot):
        for part in range(0, rows, 256):
            high, low = halves(source[part : part + 256])
            ph[slot, part : part + 256] = high
            plo[slot, part : part + 256] = low

    split_points(slab, m)

    for i in range(1, R):
        idx_copy((r + i) % R, (r + i) % R).wait_recv()

    everything = jnp.concatenate([idx[j] for j in range(R)], axis=0)
    owner = lax.shift_right_logical(everything, shift)
    local = (everything - owner * rows).astype(jnp.float32)
    owner_sel, owner_cand = owner[:, 0:ns], owner[:, ns : ns + nk]

    def ranks(mask):
        n = mask.shape[1]
        before = lax.broadcasted_iota(jnp.int32, (n, n), 0) < lax.broadcasted_iota(jnp.int32, (n, n), 1)
        return jnp.dot(
            mask.astype(jnp.bfloat16), before.astype(jnp.bfloat16), preferred_element_type=jnp.float32
        )

    def place(owners, locals_, start, packed):
        mask = jnp.where(owners == me, 1.0, 0.0)
        within = ranks(mask)
        slot = lax.broadcasted_iota(jnp.int32, (cap, mask.shape[1]), 0).astype(jnp.float32)
        for j in range(R):
            rank = jnp.where(mask[j : j + 1] > 0.0, within[j : j + 1] + start, -1.0)
            packed = packed + jnp.sum(
                jnp.where(rank == slot, locals_[j : j + 1] + 1.0, 0.0), axis=1, keepdims=True
            )
            start = start + jnp.sum(mask[j : j + 1], axis=1, keepdims=True)
        return start, packed

    start, packed = place(owner_sel, local[:, 0:ns], jnp.zeros((1, 1), jnp.float32), jnp.zeros((cap, 1), jnp.float32))
    start, packed = place(owner_cand, local[:, ns : ns + nk], start, packed)
    point = lax.broadcasted_iota(jnp.int32, (cap, rows), 1).astype(jnp.float32)
    pick = jnp.where(point == packed - 1.0, 1.0, 0.0)
    own = a * C + c
    qs[own] = jnp.dot(pick, slab[...], precision=lax.Precision.HIGHEST, preferred_element_type=jnp.float32)

    def q_copy(b, ssem, row, col):
        return remote(qs.at[b], qs.at[b], ssem.at[b], q_recv.at[b], row, col)

    def q_right(b):
        return q_copy(b, qr_send, r, c + 1)

    def q_left(b):
        return q_copy(b, ql_send, r, c - 1)

    def q_across(b, i):
        return q_copy(b, qa_send.at[i - 1], ((a + i) % A) * QUAD + m, c)

    def spread(b):
        for i in range(1, A):
            q_across(b, i).start()

    @pl.when(c + 1 < C)
    def _():
        q_right(own).start()

    @pl.when(c > 0)
    def _():
        q_left(own).start()

    spread(own)

    def split_block(b):
        high, low = halves(qs[b])
        qh[pl.ds(b * cap, cap)] = high
        ql[pl.ds(b * cap, cap)] = low

    width = 256

    def near_scores(b):
        split_block(b)

        def step(t, carry):
            slot = 2 * x + t // (rows // width)
            part = pl.ds((t % (rows // width)) * width, width)
            high, low = ph[slot, part], plo[slot, part]
            q1, q2 = qh[pl.ds(b * cap, cap)], ql[pl.ds(b * cap, cap)]
            sc[b, :, pl.ds(slot * rows + (t % (rows // width)) * width, width)] = (
                dot_nt(q1, high) + dot_nt(q2, high) + dot_nt(q1, low)
            )
            return carry

        lax.fori_loop(0, 2 * rows // width, step, 0)

    core_landed = remote(slab, pts.at[m_core], core_send.at[0], core_recv.at[0], base + m_core, c)
    core_landed.wait_recv()
    split_points(pts.at[m_core], m_core)
    near_scores(own)

    def arrive(b):
        q_copy(b, ql_send, r, c).wait_recv()

    def round_(s, carry):
        has_left = (s > 0) & (c - s >= 0)
        has_right = (s > 0) & (c + s < C)

        @pl.when(has_left)
        def _():
            b = own - s
            arrive(b)

            @pl.when(c + 1 < C)
            def _():
                q_right(b).start()

            spread(b)

        @pl.when(has_right)
        def _():
            b = own + s
            arrive(b)

            @pl.when(c > 0)
            def _():
                q_left(b).start()

            spread(b)

        @pl.when(has_left)
        def _():
            near_scores(own - s)

        @pl.when(has_right)
        def _():
            near_scores(own + s)

        x_landed(s).wait_recv()
        f_copy(s).start()

        for i in range(1, A):
            other = ((a + i) % A) * C + c

            @pl.when(c - s >= 0)
            def _():
                arrive(other - s)
                near_scores(other - s)

            @pl.when(has_right)
            def _():
                arrive(other + s)
                near_scores(other + s)

        return carry

    lax.fori_loop(0, C, round_, 0)

    def landed(s, carry):
        f_landed(s).wait_recv()
        return carry

    lax.fori_loop(0, C, landed, 0)
    split_points(pts.at[m_x], m_x)
    split_points(pts.at[m_diag], m_diag)

    def far(t, carry):
        slot = 2 * (1 - x) + t // (rows // width)
        part = pl.ds((t % (rows // width)) * width, width)
        out = pl.ds(slot * rows + (t % (rows // width)) * width, width)
        high, low = ph[slot, part], plo[slot, part]
        for b in range(0, NB, 2):
            two = slice(b * cap, (b + 2) * cap)
            value = dot_nt(qh[two], high) + dot_nt(ql[two], high) + dot_nt(qh[two], low)
            sc[b, :, out] = value[0:cap]
            sc[b + 1, :, out] = value[cap:]
        return carry

    lax.fori_loop(0, 2 * rows // width, far, 0)

    slot_id = lax.broadcasted_iota(jnp.int32, (cap, 1), 0).astype(jnp.float32)

    def largest(b, best):
        owner_id = (b % C) * R + (b // C) * QUAD + m
        count = jnp.sum(
            jnp.sum(jnp.where(owner_sel == owner_id, 1.0, 0.0), axis=1, keepdims=True), axis=0, keepdims=True
        )
        value = jnp.where(slot_id < count, sc[b], -1e30)
        return jnp.maximum(best, jnp.max(value, axis=0, keepdims=True))

    mx[m] = lax.fori_loop(0, NB, largest, jnp.full((1, span), -1e30, jnp.float32))

    def m_copy(slot, to):
        return remote(mx.at[slot], mx.at[slot], m_send.at[to], m_recv.at[slot], base + to, c)

    for i in range(1, QUAD):
        m_copy(m, (m + i) % QUAD).start()
    for i in range(1, QUAD):
        m_copy((m + i) % QUAD, (m + i) % QUAD).wait_recv()
    reached = jnp.maximum(jnp.maximum(mx[0], mx[1]), jnp.maximum(mx[2], mx[3]))
    cov[a] = jnp.maximum(cov_old[a], reached)

    def c_copy(slot, to):
        return remote(cov.at[slot], cov.at[slot], c_send.at[to], c_recv.at[slot], to * QUAD + m, c)

    for i in range(1, A):
        c_copy(a, (a + i) % A).start()

    mine = m * NB + own

    def gains(b, carry):
        total = jnp.zeros((cap, 128), jnp.float32)
        for part in range(0, span, 128):
            total = total + jnp.maximum(sc[b, :, part : part + 128] - cov[a, :, part : part + 128], 0.0)
        gr[mine, pl.ds(b, 1)] = jnp.sum(total.T, axis=0, keepdims=True)
        return carry

    lax.fori_loop(0, NB, gains, 0)

    def g_copy(slot, dev):
        return remote(gr.at[slot], gr.at[slot], g_send.at[dev], g_recv.at[slot], dev % R, dev // R)

    def g_start(i, carry):
        g_copy(mine, (me + i) % ND).start()
        return carry

    lax.fori_loop(1, ND, g_start, 0)

    mine_owner = lax.shift_right_logical(cand_col[...], shift)
    rank = jnp.zeros((nk, 1), jnp.float32)
    earlier = lax.broadcasted_iota(jnp.int32, (nk, nk), 1) < lax.broadcasted_iota(jnp.int32, (nk, nk), 0)
    for j in range(R):
        same = jnp.where(owner_sel[j : j + 1] == mine_owner, 1.0, 0.0)
        rank = rank + jnp.sum(same, axis=1, keepdims=True)
        same = jnp.where(owner_cand[j : j + 1] == mine_owner, 1.0, 0.0)
        same = jnp.where((j < r) | ((j == r) & earlier), same, 0.0)
        rank = rank + jnp.sum(same, axis=1, keepdims=True)
    row_of = mine_owner % R
    flat = (row_of % QUAD) * NB + (row_of // QUAD) * C + mine_owner // R
    pick_owner = jnp.where(lax.broadcasted_iota(jnp.int32, (nk, ND), 1) == flat, 1.0, 0.0)
    pick_slot = lax.broadcasted_iota(jnp.int32, (nk, cap), 1).astype(jnp.float32) == rank

    dev_id = lax.broadcasted_iota(jnp.int32, (ND, 1), 0)
    held = jnp.zeros((ND, 1), jnp.float32)
    for j in range(R):
        held = held + jnp.sum(jnp.where(owner_sel[j : j + 1] == dev_id, 1.0, 0.0), axis=1, keepdims=True)
        held = held + jnp.sum(jnp.where(owner_cand[j : j + 1] == dev_id, 1.0, 0.0), axis=1, keepdims=True)
    flag_out[...] = jnp.broadcast_to(jnp.max(held, axis=0, keepdims=True), flag_out.shape)

    for i in range(1, A):
        c_copy((a + i) % A, (a + i) % A).wait_recv()
    cov_out[...] = cov[...]

    def g_wait(i, carry):
        dev = (me + i) % ND
        row, col = dev % R, dev // R
        g_copy((row % QUAD) * NB + (row // QUAD) * C + col, dev).wait_recv()
        return carry

    lax.fori_loop(1, ND, g_wait, 0)
    totals = jnp.concatenate(
        [jnp.sum(gr[i * NB : (i + 1) * NB], axis=0) for i in range(QUAD)], axis=0
    )
    spread_gain = jnp.dot(pick_owner, totals, precision=lax.Precision.HIGHEST, preferred_element_type=jnp.float32)
    gain_out[...] = jnp.sum(jnp.where(pick_slot, spread_gain, 0.0), axis=1, keepdims=True)

    for i in range(1, R):
        idx_copy(r, (r + i) % R).wait_send()
    core_copy.wait_send()

    def left(s, carry):
        x_copy(s).wait_send()
        f_copy(s).wait_send()

        @pl.when(c - s >= 0)
        def _():
            @pl.when(c + 1 < C)
            def _():
                q_right(own - s).wait_send()

            for i in range(1, A):
                q_across(own - s, i).wait_send()

        @pl.when(c + s < C)
        def _():
            @pl.when(c > 0)
            def _():
                q_left(own + s).wait_send()

            @pl.when(s > 0)
            def _():
                for i in range(1, A):
                    q_across(own + s, i).wait_send()

        return carry

    lax.fori_loop(0, C, left, 0)
    for i in range(1, QUAD):
        m_copy(m, (m + i) % QUAD).wait_send()
    for i in range(1, A):
        c_copy(a, (a + i) % A).wait_send()

    def g_left(i, carry):
        g_copy(mine, (me + i) % ND).wait_send()
        return carry

    lax.fori_loop(1, ND, g_left, 0)


def fused(R, C, slab_embed, coverage_old, sel_index, cand_index):
    rows, depth = slab_embed.shape
    ns, nk = sel_index.shape[0], cand_index.shape[0]
    A, ND = R // QUAD, R * C
    NB = A * C
    span = QUAD * rows
    mean = (ns + nk) * R / ND
    cap = int(-(-mean * 1.5 // 32)) * 32
    width = -(-(ns + nk) // 128) * 128
    f32, bf16, dma = jnp.float32, jnp.bfloat16, pltpu.SemaphoreType.DMA
    vmem = pl.BlockSpec(memory_space=pltpu.VMEM)
    coverage, gain, held = pl.pallas_call(
        functools.partial(kernel, R, C, cap),
        out_shape=(
            jax.ShapeDtypeStruct((A, 1, span), f32),
            jax.ShapeDtypeStruct((nk, 1), f32),
            jax.ShapeDtypeStruct((8, 128), f32),
        ),
        in_specs=[vmem] * 5,
        out_specs=(vmem, vmem, vmem),
        scratch_shapes=[
            pltpu.VMEM((QUAD, rows, depth), f32),
            pltpu.VMEM((QUAD, rows, depth), bf16),
            pltpu.VMEM((QUAD, rows, depth), bf16),
            pltpu.VMEM((NB, cap, depth), f32),
            pltpu.VMEM((NB * cap, depth), bf16),
            pltpu.VMEM((NB * cap, depth), bf16),
            pltpu.VMEM((NB, cap, span), f32),
            pltpu.VMEM((R, 1, width), jnp.int32),
            pltpu.VMEM((QUAD, 1, span), f32),
            pltpu.VMEM((A, 1, span), f32),
            pltpu.VMEM((8, 128), f32),
            pltpu.VMEM((ND, NB, cap), f32),
            dma((R,)), dma((R,)), dma((1,)), dma((1,)), dma((C,)), dma((C,)), dma((C,)), dma((C,)),
            dma((NB,)), dma((NB,)), dma((NB,)), dma((A - 1, NB)),
            dma((QUAD,)), dma((QUAD,)), dma((A,)), dma((A,)), dma((ND,)), dma((ND,)),
        ],
        compiler_params=pltpu.CompilerParams(
            collective_id=0, has_side_effects=True, vmem_limit_bytes=58 * 1024 * 1024
        ),
        cost_estimate=pl.CostEstimate(
            flops=6 * NB * cap * span * depth, bytes_accessed=rows * depth * 4, transcendentals=0
        ),
    )(
        slab_embed,
        coverage_old.reshape(A, 1, span),
        sel_index.reshape(1, ns),
        cand_index.reshape(1, nk),
        cand_index.reshape(nk, 1),
    )
    return coverage.reshape(A * span), gain.reshape(nk), held[0, 0] > cap


def body(R, C, slab_embed, coverage_old, sel_index, cand_index):
    coverage, gain, crowded = fused(R, C, slab_embed, coverage_old, sel_index, cand_index)
    return lax.cond(
        crowded,
        lambda: any_draw(slab_embed, coverage_old, sel_index, cand_index),
        lambda: (coverage, gain),
    )


def solution(mesh):
    in_specs = (P(("col", "row"), None), P("col"), P("row"), P("row"))
    out_specs = (P("col"), P("row"))
    return jax.shard_map(
        functools.partial(body, mesh.shape["row"], mesh.shape["col"]),
        mesh=mesh, in_specs=in_specs, out_specs=out_specs, check_vma=False,
    )
```

time: 222 us -> 103 us (0.46)
  waiting for transfers between devices: 126 us -> 0 us
  Pallas kernels: 0 us -> 83.9 us
  blocking collectives: 34.8 us -> 0 us
  matrix products: 31.7 us -> 0 us
  local copies, waits for them, and re-layouts: 11.3 us -> 4.05 us
  other arithmetic: 3.22 us -> 0 us
    pallas_call x0 -> x1, Pallas kernels: none -> 83.9 us  [fused(): pl.pallas_call(functools.partial(kernel, R, C, cap), out_shape=(jax.Shape...]
    all_gather x1 -> x0, waiting for transfers between devices: 75.4 us -> none  [body(): gathered = lax.all_gather(slab_embed, 'row', axis=0, tiled=True)]
    psum x1 -> x0, waiting for transfers between devices: 50.3 us -> none  [body(): lax.psum((lookup(gathered, sel_index, first_row), lookup(gathered, cand_i...]
    dot_general x2 -> x0, matrix products: 31.7 us -> none  [similar(): lax.dot_general(left, right, (((1,), (1,)), ((), ())), precision=lax.Prec...]
    pmax x1 -> x0, blocking collectives: 24.2 us -> none  [body(): reached = lax.pmax(partial_value, 'row')]
    gather x2 -> x0, local copies, waits for them, and re-layouts: 11.3 us -> none  [lookup(): jnp.take(source, jnp.clip(position, 0, source.shape[0] - 1), axis=0)]
    psum x1 -> x0, blocking collectives: 10.6 us -> none  [body(): total_gain = lax.psum(gain_part, 'col')]
  transfers between devices with their start and end apart: 2 -> 0, of which waited for: 2 -> 0; matrix products, arithmetic and copies ran while one was open for 1% -> 0% of each run, Pallas kernels for 0% -> 0%
where the time goes in v1:
time: 103 us
  Pallas kernels  83.9 us (81%)
  between operations  14.7 us (14%)
  local copies, waits for them, and re-layouts  4.05 us (4%)
    pallas_call x1, Pallas kernels, fused(): pl.pallas_call(functools.partial(kernel, R, C, cap), out_shape=(jax.Shape...  83.9 us

profile of v1, /device:TPU:0, one launch (start us, length us, event | category | flops | bytes accessed | tf_op | source)
XLA Modules:
  0.0 102.9 jit_solution(6519697275326007920)
XLA Ops:
  7.2 1.4 %copy.11.cand_col = s32[192,1]{1,0:T(8,128)} copy(s32[192,1]{0,1:T(1,128)} %bitcast.12) | data formatting | bytes 1536 | tf_op jit(solution)/shard_map/reshape | solution.py:478
  8.6 0.0 copy-start.1
  8.6 0.0 copy-start.2
  8.6 0.0 copy-start.4
  8.6 83.9 %shard_map.63 = (f32[2,1,2048]{2,1,0:T(1,128)}, f32[192,1]{1,0:T(8,128)S(1)}, f32[8,128]{1,0:T(8,128)}) custom-call(f32[512,768]{1,0:T(8,128)} %slab.1, f32[2,1,2048]{2,1,0:T(1,128)} %bitcast.11, s32[1,128]{1,0:T(1,128)} %bitcast.15, s32[1,192]{1,0:T(1,128)} %bitcast.13, s32[192,1]{1,0:T(8,128)} %copy.11.cand_col), custom_call_target="tpu_custom_call" | custom-call | flops 9663676416 | bytes 1572864 | tf_op jit(solution)/shard_map/pallas_call | solution.py:441
  92.6 1.2 %slice.3 = f32[1,1]{1,0:T(1,128)} slice(f32[8,128]{1,0:T(8,128)} %get-tuple-element.27), slice={[0:1], [0:1]} | slice | bytes 8 | tf_op jit(solution)/shard_map/slice | solution.py:480
  94.4 0.0 copy-done.1
  94.4 0.0 copy-done.2
  94.4 0.0 copy-done.4
  94.4 0.3 conditional.1
  94.4 0.1 copy.12
  94.7 0.0 copy-start.3
  94.7 1.3 %copy.20 = f32[4096]{0:T(1024)} copy(f32[4096]{0:T(1024)} %get-tuple-element.50) | data formatting | bytes 32768
  96.0 0.0 copy-done.3
Async XLA Ops:
  8.6 85.8 %copy-start.1 = (f32[4096]{0:T(1024)S(1)}, f32[4096]{0:T(1024)}, u32[]{:S(2)}) copy-start(f32[4096]{0:T(1024)} %param.7) | copy-start | bytes 49156
  8.6 85.8 %copy-start.2 = (s32[192]{0:T(256)S(1)}, s32[192]{0:T(256)}, u32[]{:S(2)}) copy-start(s32[192]{0:T(256)} %param.9) | copy-start | bytes 2308
  8.6 85.8 %copy-start.4 = (s32[128]{0:T(128)S(1)}, s32[128]{0:T(128)}, u32[]{:S(2)}) copy-start(s32[128]{0:T(128)} %param.8) | copy-start | bytes 1540
  94.7 1.3 %copy-start.3 = (f32[192]{0:T(256)}, f32[192]{0:T(256)S(1)}, u32[]{:S(2)}) copy-start(f32[192]{0:T(256)S(1)} %get-tuple-element.51) | copy-start | bytes 2308

commit v2 on v1

v2 whole, which is shorter than its diff:
```python
import functools

import jax
import jax.numpy as jnp
from jax import lax
from jax.experimental import pallas as pl
from jax.experimental.pallas import tpu as pltpu
from jax.sharding import PartitionSpec as P

MESH = pl.DeviceIdType.MESH
QUAD = 4
NT = (((1,), (1,)), ((), ()))


def similar(left, right):
    return lax.dot_general(
        left,
        right,
        (((1,), (1,)), ((), ())),
        precision=lax.Precision.HIGHEST,
        preferred_element_type=jnp.float32,
    )


def lookup(source, indices, first_row):
    position = indices - first_row
    inside = (position >= 0) & (position < source.shape[0])
    picked = jnp.take(source, jnp.clip(position, 0, source.shape[0] - 1), axis=0)
    return jnp.where(inside[:, None], picked, 0.0)


def any_draw(slab_embed, coverage_old, sel_index, cand_index):
    col_id = lax.axis_index("col")
    gathered = lax.all_gather(slab_embed, "row", axis=0, tiled=True)
    first_row = col_id * gathered.shape[0]
    selected, chosen = lax.psum(
        (lookup(gathered, sel_index, first_row), lookup(gathered, cand_index, first_row)), "col"
    )
    partial_value = jnp.max(similar(selected, gathered), axis=0)
    reached = lax.pmax(partial_value, "row")
    coverage = jnp.maximum(coverage_old, reached)
    gain_part = jnp.sum(jnp.maximum(similar(chosen, gathered) - coverage[None, :], 0.0), axis=1)
    return coverage, lax.psum(gain_part, "col")


def halves(value):
    high = value.astype(jnp.bfloat16)
    return high, (value - high.astype(jnp.float32)).astype(jnp.bfloat16)


def dot_nt(left, right):
    return lax.dot_general(left, right, NT, preferred_element_type=jnp.float32)


def kernel(
    R, C, cap, slab, cov_old, sel, cand,
    cov_out, gain_out, flag_out,
    pts, ph, plo, qs, qh, ql, sc, idx, bias, best, mx, cov, gr,
    idx_send, idx_recv, core_send, core_recv, x_send, x_recv, f_send, f_recv,
    q_recv, ql_send, qr_send, qa_send, m_send, m_recv, c_send, c_recv, g_send, g_recv,
):
    A = R // QUAD
    NB = A * C
    ND = R * C
    rows = slab.shape[0]
    ns, nk = sel.shape[1], cand.shape[1]
    shift = rows.bit_length() - 1
    span = QUAD * rows
    r = lax.axis_index("row")
    c = lax.axis_index("col")
    me = c * R + r
    a = lax.div(r, QUAD)
    m = lax.rem(r, QUAD)
    x, h = lax.div(m, 2), lax.rem(m, 2)
    m_core = 2 * x + (1 - h)
    m_x = 2 * (1 - x) + h
    m_diag = 2 * (1 - x) + (1 - h)
    base = a * QUAD
    width = 256
    parts = rows // width

    def remote(src, dst, ssem, rsem, row, col):
        return pltpu.make_async_remote_copy(
            src_ref=src, dst_ref=dst, send_sem=ssem, recv_sem=rsem,
            device_id=(row, col), device_id_type=MESH,
        )

    barrier = pltpu.get_barrier_semaphore()

    def greet(i, carry):
        dev = lax.rem(me + i, ND)
        pl.semaphore_signal(barrier, inc=1, device_id=(lax.rem(dev, R), lax.div(dev, R)), device_id_type=MESH)
        return carry

    lax.fori_loop(1, ND, greet, 0)
    idx[r] = jnp.full(idx.shape[1:], -1, jnp.int32)
    idx[r, :, 0:ns] = sel[...]
    idx[r, :, ns : ns + nk] = cand[...]
    pl.semaphore_wait(barrier, ND - 1)

    def idx_copy(slot, to):
        return remote(idx.at[slot], idx.at[slot], idx_send.at[to], idx_recv.at[slot], to, c)

    for i in range(1, R):
        idx_copy(r, lax.rem(r + i, R)).start()

    core_copy = remote(slab, pts.at[m], core_send.at[0], core_recv.at[0], base + m_core, c)
    core_copy.start()

    def x_copy(s):
        part = pl.ds(s * width, width)
        return remote(slab.at[part], pts.at[m, part], x_send.at[s], x_recv.at[s], base + m_x, c)

    def x_landed(s):
        part = pl.ds(s * width, width)
        return remote(slab.at[part], pts.at[m_x, part], x_send.at[s], x_recv.at[s], base + m_x, c)

    def f_copy(s):
        part = pl.ds(s * width, width)
        return remote(pts.at[m_x, part], pts.at[m_x, part], f_send.at[s], f_recv.at[s], base + m_core, c)

    def f_landed(s):
        part = pl.ds(s * width, width)
        return remote(pts.at[m_diag, part], pts.at[m_diag, part], f_send.at[s], f_recv.at[s], base + m_core, c)

    for s in range(parts):
        x_copy(s).start()

    def split_part(source, slot, s):
        part = pl.ds(s * width, width)
        high, low = halves(source[part])
        ph[slot, part] = high
        plo[slot, part] = low

    def split_points(source, slot):
        for s in range(parts):
            split_part(source, slot, s)

    best[...] = jnp.full(best.shape, -1e30, jnp.float32)
    split_points(slab, m)

    for i in range(1, R):
        idx_copy(lax.rem(r + i, R), lax.rem(r + i, R)).wait_recv()

    everything = jnp.concatenate([idx[j] for j in range(R)], axis=0)
    owner = lax.shift_right_logical(everything, shift)
    local = (everything - owner * rows).astype(jnp.float32)
    owner_sel, owner_cand = owner[:, 0:ns], owner[:, ns:]
    slot_id = lax.broadcasted_iota(jnp.int32, (cap, 128), 0).astype(jnp.float32)

    def place(owners, locals_, start, packed):
        n = owners.shape[1]
        mask = jnp.where(owners == me, 1.0, 0.0)
        before = lax.broadcasted_iota(jnp.int32, (n, n), 0) < lax.broadcasted_iota(jnp.int32, (n, n), 1)
        within = jnp.dot(
            mask.astype(jnp.bfloat16), before.astype(jnp.bfloat16), preferred_element_type=jnp.float32
        )
        for j in range(R):
            rank = jnp.where(mask[j : j + 1] > 0.0, within[j : j + 1] + start, -1.0)
            spot = locals_[j : j + 1] + 1.0
            for lane in range(0, n, 128):
                packed = packed + jnp.where(
                    rank[:, lane : lane + 128] == slot_id, spot[:, lane : lane + 128], 0.0
                )
            start = start + jnp.sum(mask[j : j + 1], axis=1, keepdims=True)
        return start, packed

    start, packed = place(
        owner_sel, local[:, 0:ns], jnp.zeros((1, 1), jnp.float32), jnp.zeros((cap, 128), jnp.float32)
    )
    start, packed = place(owner_cand, local[:, ns:], start, packed)
    packed = jnp.sum(packed, axis=1, keepdims=True)
    point = lax.broadcasted_iota(jnp.int32, (cap, rows), 1).astype(jnp.float32)
    pick = jnp.where(point == packed - 1.0, 1.0, 0.0)
    own = a * C + c
    qs[own] = jnp.dot(pick, slab[...], precision=lax.Precision.HIGHEST, preferred_element_type=jnp.float32)

    def q_copy(b, ssem, row, col):
        return remote(qs.at[b], qs.at[b], ssem.at[b], q_recv.at[b], row, col)

    def q_right(b):
        return q_copy(b, qr_send, r, c + 1)

    def q_left(b):
        return q_copy(b, ql_send, r, c - 1)

    def q_across(b, i):
        return q_copy(b, qa_send.at[i - 1], (lax.rem(a + i, A)) * QUAD + m, c)

    def spread(b):
        for i in range(1, A):
            q_across(b, i).start()

    @pl.when(c + 1 < C)
    def _():
        q_right(own).start()

    @pl.when(c > 0)
    def _():
        q_left(own).start()

    spread(own)

    def split_block(b):
        high, low = halves(qs[b])
        qh[pl.ds(b * cap, cap)] = high
        ql[pl.ds(b * cap, cap)] = low

    def score(first, count, slot, s):
        part = pl.ds(s * width, width)
        out = pl.ds(slot * rows + s * width, width)
        block = pl.ds(first * cap, count * cap)
        high, low = ph[slot, part], plo[slot, part]
        value = dot_nt(qh[block], high) + dot_nt(ql[block], high) + dot_nt(qh[block], low)
        sc[block, out] = value
        shift_by = bias[block]
        top = jnp.concatenate(
            [
                jnp.max(
                    (value[:, lane : lane + 128] + shift_by).reshape(count * cap // 8, 8, 128), axis=0
                )
                for lane in range(0, width, 128)
            ],
            axis=1,
        )
        best[:, out] = jnp.maximum(best[:, out], top)

    def near_scores(b):
        split_block(b)

        def step(t, carry):
            score(b, 1, 2 * x + lax.div(t, parts), lax.rem(t, parts))
            return carry

        lax.fori_loop(0, 2 * parts, step, 0)

    core_landed = remote(slab, pts.at[m_core], core_send.at[0], core_recv.at[0], base + m_core, c)
    core_landed.wait_recv()
    split_points(pts.at[m_core], m_core)
    def mark(b, carry):
        owner_id = lax.rem(b, C) * R + lax.div(b, C) * QUAD + m
        count = jnp.sum(
            jnp.sum(jnp.where(owner_sel == owner_id, 1.0, 0.0), axis=1, keepdims=True), axis=0, keepdims=True
        )
        bias[pl.ds(b * cap, cap)] = jnp.where(slot_id < count, 0.0, -1e30)
        return carry

    lax.fori_loop(0, NB, mark, 0)
    near_scores(own)

    square = (nk, nk)
    across, down = lax.broadcasted_iota(jnp.int32, square, 1), lax.broadcasted_iota(jnp.int32, square, 0)
    mine_row = lax.shift_right_logical(cand[...], shift).astype(jnp.float32)
    mine_owner = jnp.sum(jnp.where(across == down, mine_row, 0.0), axis=1, keepdims=True).astype(jnp.int32)
    wide = owner_cand.shape[1]
    earlier = lax.broadcasted_iota(jnp.int32, (nk, wide), 1) < lax.broadcasted_iota(jnp.int32, (nk, wide), 0)
    same_total = jnp.zeros((nk, 128), jnp.float32)
    for j in range(R):
        same = jnp.where(owner_sel[j : j + 1] == mine_owner, 1.0, 0.0)
        for lane in range(0, ns, 128):
            same_total = same_total + same[:, lane : lane + 128]
        counted = (j < r) | ((j == r) & earlier)
        same = jnp.where(counted & (owner_cand[j : j + 1] == mine_owner), 1.0, 0.0)
        for lane in range(0, wide, 128):
            same_total = same_total + same[:, lane : lane + 128]
    rank = jnp.sum(same_total, axis=1, keepdims=True)
    row_of = lax.rem(mine_owner, R)
    flat = lax.rem(row_of, QUAD) * NB + lax.div(row_of, QUAD) * C + lax.div(mine_owner, R)
    pick_owner = jnp.where(lax.broadcasted_iota(jnp.int32, (nk, ND), 1) == flat, 1.0, 0.0)
    pick_slot = lax.broadcasted_iota(jnp.int32, (nk, cap), 1).astype(jnp.float32) == rank

    dev_id = lax.broadcasted_iota(jnp.int32, (ND, 1), 0)
    held = jnp.zeros((ND, 128), jnp.float32)
    for j in range(R):
        for lane in range(0, ns + wide, 128):
            held = held + jnp.where(owner[j : j + 1, lane : lane + 128] == dev_id, 1.0, 0.0)
    held = jnp.sum(held, axis=1, keepdims=True)
    flag_out[...] = jnp.max(held, axis=0, keepdims=True)

    def arrive(b):
        q_copy(b, ql_send, r, c).wait_recv()

    def across_blocks(s):
        for i in range(1, A):
            other = lax.rem(a + i, A) * C + c

            @pl.when(c - s >= 0)
            def _():
                arrive(other - s)
                near_scores(other - s)

            @pl.when((s > 0) & (c + s < C))
            def _():
                arrive(other + s)
                near_scores(other + s)

    def round_(s, carry):
        has_left = (s < C) & (c - s >= 0)
        has_right = (s < C) & (c + s < C)

        @pl.when(has_left)
        def _():
            b = own - s
            arrive(b)

            @pl.when(c + 1 < C)
            def _():
                q_right(b).start()

            spread(b)

        @pl.when(has_right)
        def _():
            b = own + s
            arrive(b)

            @pl.when(c > 0)
            def _():
                q_left(b).start()

            spread(b)

        @pl.when(has_left)
        def _():
            near_scores(own - s)

        @pl.when(has_right)
        def _():
            near_scores(own + s)

        @pl.when(s == C)
        def _():
            for t in range(parts):
                x_landed(t).wait_recv()
                f_copy(t).start()

            def step(t, carry):
                split_part(pts.at[m_x], m_x, t)
                score(a * C, C, m_x, t)
                return carry

            lax.fori_loop(0, parts, step, 0)

        across_blocks(s - 1)
        return carry

    lax.fori_loop(1, C + 1, round_, 0)
    for t in range(parts):
        f_landed(t).wait_recv()
        split_part(pts.at[m_diag], m_diag, t)

    def far(t, carry):
        score(a * C, C, m_diag, t)
        return carry

    lax.fori_loop(0, parts, far, 0)
    for i in range(1, A):
        other = lax.rem(a + i, A) * C

        def far_across(t, carry):
            score(other, C, 2 * (1 - x) + lax.div(t, parts), lax.rem(t, parts))
            return carry

        lax.fori_loop(0, 2 * parts, far_across, 0)

    mx[m] = jnp.max(best[...], axis=0, keepdims=True)

    def m_copy(slot, to):
        return remote(mx.at[slot], mx.at[slot], m_send.at[to], m_recv.at[slot], base + to, c)

    for i in range(1, QUAD):
        m_copy(m, lax.rem(m + i, QUAD)).start()
    for i in range(1, QUAD):
        m_copy(lax.rem(m + i, QUAD), lax.rem(m + i, QUAD)).wait_recv()
    reached = jnp.maximum(jnp.maximum(mx[0], mx[1]), jnp.maximum(mx[2], mx[3]))
    cov[a] = jnp.maximum(cov_old[a], reached)

    def c_copy(slot, to):
        return remote(cov.at[slot], cov.at[slot], c_send.at[to], c_recv.at[slot], to * QUAD + m, c)

    for i in range(1, A):
        c_copy(a, lax.rem(a + i, A)).start()

    mine = m * NB + own

    def gains(b, carry):
        total = jnp.zeros((cap, 128), jnp.float32)
        for part in range(0, span, 128):
            total = total + jnp.maximum(sc[pl.ds(b * cap, cap), part : part + 128] - cov[a, :, part : part + 128], 0.0)
        gr[mine, pl.ds(b, 1)] = jnp.sum(total.T, axis=0, keepdims=True)
        return carry

    lax.fori_loop(0, NB, gains, 0)

    def g_copy(slot, dev):
        return remote(
            gr.at[slot], gr.at[slot], g_send.at[dev], g_recv.at[slot], lax.rem(dev, R), lax.div(dev, R)
        )

    def g_start(i, carry):
        g_copy(mine, lax.rem(me + i, ND)).start()
        return carry

    lax.fori_loop(1, ND, g_start, 0)

    for i in range(1, A):
        c_copy(lax.rem(a + i, A), lax.rem(a + i, A)).wait_recv()
    cov_out[...] = cov[...]

    def g_wait(i, carry):
        dev = lax.rem(me + i, ND)
        row, col = lax.rem(dev, R), lax.div(dev, R)
        g_copy(lax.rem(row, QUAD) * NB + lax.div(row, QUAD) * C + col, dev).wait_recv()
        return carry

    lax.fori_loop(1, ND, g_wait, 0)
    totals = jnp.concatenate(
        [jnp.sum(gr[i * NB : (i + 1) * NB], axis=0) for i in range(QUAD)], axis=0
    )
    spread_gain = jnp.dot(pick_owner, totals, precision=lax.Precision.HIGHEST, preferred_element_type=jnp.float32)
    gain_out[...] = jnp.sum(jnp.where(pick_slot, spread_gain, 0.0), axis=1, keepdims=True)

    for i in range(1, R):
        idx_copy(r, lax.rem(r + i, R)).wait_send()
    core_copy.wait_send()

    for s in range(parts):
        x_copy(s).wait_send()
        f_copy(s).wait_send()

    def left(s, carry):
        @pl.when(c - s >= 0)
        def _():
            @pl.when(c + 1 < C)
            def _():
                q_right(own - s).wait_send()

            for i in range(1, A):
                q_across(own - s, i).wait_send()

        @pl.when(c + s < C)
        def _():
            @pl.when(c > 0)
            def _():
                q_left(own + s).wait_send()

            @pl.when(s > 0)
            def _():
                for i in range(1, A):
                    q_across(own + s, i).wait_send()

        return carry

    lax.fori_loop(0, C, left, 0)
    for i in range(1, QUAD):
        m_copy(m, lax.rem(m + i, QUAD)).wait_send()
    for i in range(1, A):
        c_copy(a, lax.rem(a + i, A)).wait_send()

    def g_left(i, carry):
        g_copy(mine, lax.rem(me + i, ND)).wait_send()
        return carry

    lax.fori_loop(1, ND, g_left, 0)


def fused(R, C, slab_embed, coverage_old, sel_index, cand_index):
    rows, depth = slab_embed.shape
    ns, nk = sel_index.shape[0], cand_index.shape[0]
    A, ND = R // QUAD, R * C
    NB = A * C
    span = QUAD * rows
    mean = (ns + nk) * R / ND
    cap = int(-(-mean * 1.5 // 32)) * 32
    width = -(-(ns + nk) // 128) * 128
    parts = rows // 256
    f32, bf16, dma = jnp.float32, jnp.bfloat16, pltpu.SemaphoreType.DMA
    vmem = pl.BlockSpec(memory_space=pltpu.VMEM)
    coverage, gain, held = pl.pallas_call(
        functools.partial(kernel, R, C, cap),
        out_shape=(
            jax.ShapeDtypeStruct((A, 1, span), f32),
            jax.ShapeDtypeStruct((nk, 1), f32),
            jax.ShapeDtypeStruct((1, 1), f32),
        ),
        in_specs=[vmem] * 4,
        out_specs=(vmem, vmem, vmem),
        scratch_shapes=[
            pltpu.VMEM((QUAD, rows, depth), f32),
            pltpu.VMEM((QUAD, rows, depth), bf16),
            pltpu.VMEM((QUAD, rows, depth), bf16),
            pltpu.VMEM((NB, cap, depth), f32),
            pltpu.VMEM((NB * cap, depth), bf16),
            pltpu.VMEM((NB * cap, depth), bf16),
            pltpu.VMEM((NB * cap, span), f32),
            pltpu.VMEM((R, 1, width), jnp.int32),
            pltpu.VMEM((NB * cap, 128), f32),
            pltpu.VMEM((8, span), f32),
            pltpu.VMEM((QUAD, 1, span), f32),
            pltpu.VMEM((A, 1, span), f32),
            pltpu.VMEM((ND, NB, cap), f32),
            dma((R,)), dma((R,)), dma((1,)), dma((1,)),
            dma((parts,)), dma((parts,)), dma((parts,)), dma((parts,)),
            dma((NB,)), dma((NB,)), dma((NB,)), dma((A - 1, NB)),
            dma((QUAD,)), dma((QUAD,)), dma((A,)), dma((A,)), dma((ND,)), dma((ND,)),
        ],
        compiler_params=pltpu.CompilerParams(
            collective_id=0, has_side_effects=True, vmem_limit_bytes=58 * 1024 * 1024
        ),
        cost_estimate=pl.CostEstimate(
            flops=6 * NB * cap * span * depth, bytes_accessed=rows * depth * 4, transcendentals=0
        ),
    )(
        slab_embed,
        coverage_old.reshape(A, 1, span),
        sel_index.reshape(1, ns),
        cand_index.reshape(1, nk),
    )
    return coverage.reshape(A * span), gain.reshape(nk), held[0, 0] > cap


def body(R, C, slab_embed, coverage_old, sel_index, cand_index):
    coverage, gain, crowded = fused(R, C, slab_embed, coverage_old, sel_index, cand_index)
    return lax.cond(
        crowded,
        lambda: any_draw(slab_embed, coverage_old, sel_index, cand_index),
        lambda: (coverage, gain),
    )


def solution(mesh):
    in_specs = (P(("col", "row"), None), P("col"), P("row"), P("row"))
    out_specs = (P("col"), P("row"))
    return jax.shard_map(
        functools.partial(body, mesh.shape["row"], mesh.shape["col"]),
        mesh=mesh, in_specs=in_specs, out_specs=out_specs, check_vma=False,
    )
```

time: 103 us -> 86.6 us (0.84)
  Pallas kernels: 83.9 us -> 70 us
  local copies, waits for them, and re-layouts: 4.05 us -> 1.42 us
    pallas_call x1, Pallas kernels: 83.9 us -> 70 us  [fused(): pl.pallas_call(functools.partial(kernel, R, C, cap), out_shape=(jax.Shape...]
    reshape x1 -> x0, local copies, waits for them, and re-layouts: 1.44 us -> none  [fused(): cand_index.reshape(nk, 1)]
    slice x1 -> x0, local copies, waits for them, and re-layouts: 1.19 us -> none  [fused(): return (coverage.reshape(A * span), gain.reshape(nk), held[0, 0] > cap)]
where the time goes in v2:
time: 86.6 us; the launch traced here: 86.3 us
  Pallas kernels  70 us (81%)
  between operations  14.7 us (17%)
  local copies, waits for them, and re-layouts  1.42 us (2%)
    pallas_call x1, Pallas kernels, fused(): pl.pallas_call(functools.partial(kernel, R, C, cap), out_shape=(jax.Shape...  70 us

profile of v2, /device:TPU:0, one launch (start us, length us, event | category | flops | bytes accessed | tf_op | source)
XLA Modules:
  0.0 86.3 jit_solution(8954429789388111168)
XLA Ops:
  7.2 0.0 copy-start.1
  7.2 0.0 copy-start.3
  7.2 0.0 copy-start.4
  7.2 70.0 %shard_map.63 = (f32[2,1,2048]{2,1,0:T(1,128)}, f32[192,1]{1,0:T(8,128)S(1)}, f32[1,1]{1,0:T(1,128)}) custom-call(f32[512,768]{1,0:T(8,128)} %slab.1, f32[2,1,2048]{2,1,0:T(1,128)} %bitcast.10, s32[1,128]{1,0:T(1,128)} %bitcast.13, s32[1,192]{1,0:T(1,128)} %bitcast.12), custom_call_target="tpu_custom_call" | custom-call | flops 9663676416 | bytes 1572864 | tf_op jit(solution)/shard_map/pallas_call | solution.py:479
  77.8 0.0 copy-done.1
  77.9 0.0 copy-done.3
  77.9 0.0 copy-done.4
  77.9 0.3 conditional.1
  77.9 0.1 copy.10
  78.2 0.0 copy-start.2
  78.2 1.3 %copy.18 = f32[4096]{0:T(1024)} copy(f32[4096]{0:T(1024)} %get-tuple-element.48) | data formatting | bytes 32768
  79.5 0.0 copy-done.2
Async XLA Ops:
  7.2 70.7 %copy-start.1 = (f32[4096]{0:T(1024)S(1)}, f32[4096]{0:T(1024)}, u32[]{:S(2)}) copy-start(f32[4096]{0:T(1024)} %param.7) | copy-start | bytes 49156
  7.2 70.7 %copy-start.3 = (s32[192]{0:T(256)S(1)}, s32[192]{0:T(256)}, u32[]{:S(2)}) copy-start(s32[192]{0:T(256)} %param.9) | copy-start | bytes 2308
  7.2 70.7 %copy-start.4 = (s32[128]{0:T(128)S(1)}, s32[128]{0:T(128)}, u32[]{:S(2)}) copy-start(s32[128]{0:T(128)} %param.8) | copy-start | bytes 1540
  78.2 1.3 %copy-start.2 = (f32[192]{0:T(256)}, f32[192]{0:T(256)S(1)}, u32[]{:S(2)}) copy-start(f32[192]{0:T(256)S(1)} %get-tuple-element.49) | copy-start | bytes 2308

commit v3 on v2

--- a/solution.py
+++ b/solution.py
@@ -53,7 +53,7 @@
 
 
 def kernel(
-    R, C, cap, slab, cov_old, sel, cand,
+    R, C, cap, sent, slab, cov_old, sel, cand,
     cov_out, gain_out, flag_out,
     pts, ph, plo, qs, qh, ql, sc, idx, bias, best, mx, cov, gr,
     idx_send, idx_recv, core_send, core_recv, x_send, x_recv, f_send, f_recv,
@@ -136,6 +136,8 @@
         for s in range(parts):
             split_part(source, slot, s)
 
+    if sent < cap:
+        qs[:, sent:] = jnp.zeros((NB, cap - sent, qs.shape[2]), jnp.float32)
     best[...] = jnp.full(best.shape, -1e30, jnp.float32)
     split_points(slab, m)
 
@@ -173,10 +175,12 @@
     point = lax.broadcasted_iota(jnp.int32, (cap, rows), 1).astype(jnp.float32)
     pick = jnp.where(point == packed - 1.0, 1.0, 0.0)
     own = a * C + c
-    qs[own] = jnp.dot(pick, slab[...], precision=lax.Precision.HIGHEST, preferred_element_type=jnp.float32)
+    rows_owned = jnp.dot(pick, slab[...], precision=lax.Precision.HIGHEST, preferred_element_type=jnp.float32)
+    qs[own, 0:sent] = rows_owned[0:sent]
 
     def q_copy(b, ssem, row, col):
-        return remote(qs.at[b], qs.at[b], ssem.at[b], q_recv.at[b], row, col)
+        part = qs.at[b, pl.ds(0, sent)]
+        return remote(part, part, ssem.at[b], q_recv.at[b], row, col)
 
     def q_right(b):
         return q_copy(b, qr_send, r, c + 1)
@@ -211,13 +215,15 @@
         out = pl.ds(slot * rows + s * width, width)
         block = pl.ds(first * cap, count * cap)
         high, low = ph[slot, part], plo[slot, part]
-        value = dot_nt(qh[block], high) + dot_nt(ql[block], high) + dot_nt(qh[block], low)
+        n = count * cap
+        both = dot_nt(jnp.concatenate([qh[block], ql[block]], axis=0), high)
+        value = both[0:n] + both[n:] + dot_nt(qh[block], low)
         sc[block, out] = value
         shift_by = bias[block]
         top = jnp.concatenate(
             [
                 jnp.max(
-                    (value[:, lane : lane + 128] + shift_by).reshape(count * cap // 8, 8, 128), axis=0
+                    (value[:, lane : lane + 128] + shift_by).reshape(n // 8, 8, 128), axis=0
                 )
                 for lane in range(0, width, 128)
             ],
@@ -328,7 +334,7 @@
         def _():
             near_scores(own + s)
 
-        @pl.when(s == C)
+        @pl.when(s == C - 1)
         def _():
             for t in range(parts):
                 x_landed(t).wait_recv()
@@ -341,19 +347,22 @@
 
             lax.fori_loop(0, parts, step, 0)
 
+        @pl.when(s == C)
+        def _():
+            for t in range(parts):
+                f_landed(t).wait_recv()
+
+            def step(t, carry):
+                split_part(pts.at[m_diag], m_diag, t)
+                score(a * C, C, m_diag, t)
+                return carry
+
+            lax.fori_loop(0, parts, step, 0)
+
         across_blocks(s - 1)
         return carry
 
     lax.fori_loop(1, C + 1, round_, 0)
-    for t in range(parts):
-        f_landed(t).wait_recv()
-        split_part(pts.at[m_diag], m_diag, t)
-
-    def far(t, carry):
-        score(a * C, C, m_diag, t)
-        return carry
-
-    lax.fori_loop(0, parts, far, 0)
     for i in range(1, A):
         other = lax.rem(a + i, A) * C
 
@@ -471,13 +480,14 @@
     NB = A * C
     span = QUAD * rows
     mean = (ns + nk) * R / ND
-    cap = int(-(-mean * 1.5 // 32)) * 32
+    sent = int(-(-(mean + 3.7 * mean**0.5) // 8)) * 8
+    cap = -(-sent // 32) * 32
     width = -(-(ns + nk) // 128) * 128
     parts = rows // 256
     f32, bf16, dma = jnp.float32, jnp.bfloat16, pltpu.SemaphoreType.DMA
     vmem = pl.BlockSpec(memory_space=pltpu.VMEM)
     coverage, gain, held = pl.pallas_call(
-        functools.partial(kernel, R, C, cap),
+        functools.partial(kernel, R, C, cap, sent),
         out_shape=(
             jax.ShapeDtypeStruct((A, 1, span), f32),
             jax.ShapeDtypeStruct((nk, 1), f32),
@@ -516,7 +526,7 @@
         sel_index.reshape(1, ns),
         cand_index.reshape(1, nk),
     )
-    return coverage.reshape(A * span), gain.reshape(nk), held[0, 0] > cap
+    return coverage.reshape(A * span), gain.reshape(nk), held[0, 0] > sent
 
 
 def body(R, C, slab_embed, coverage_old, sel_index, cand_index):

time: 86.6 us -> 81.3 us (0.939)
  Pallas kernels: 70 us -> 64.8 us
    pallas_call x1, Pallas kernels: 70 us -> 64.8 us  [fused(): pl.pallas_call(functools.partial(kernel, R, C, cap, sent), out_shape=(jax...]
where the time goes in v3:
time: 81.3 us; the launch traced here: 81.1 us
  Pallas kernels  64.8 us (80%)
  between operations  14.7 us (18%)
  local copies, waits for them, and re-layouts  1.42 us (2%)
    pallas_call x1, Pallas kernels, fused(): pl.pallas_call(functools.partial(kernel, R, C, cap, sent), out_shape=(jax...  64.8 us

profile of v3, /device:TPU:0, one launch (start us, length us, event | category | flops | bytes accessed | tf_op | source)
XLA Modules:
  0.0 81.1 jit_solution(12642811152062691532)
XLA Ops:
  7.2 0.0 copy-start.1
  7.2 0.0 copy-start.3
  7.2 0.0 copy-start.4
  7.2 64.8 %shard_map.63 = (f32[2,1,2048]{2,1,0:T(1,128)}, f32[192,1]{1,0:T(8,128)S(1)}, f32[1,1]{1,0:T(1,128)}) custom-call(f32[512,768]{1,0:T(8,128)} %slab.1, f32[2,1,2048]{2,1,0:T(1,128)} %bitcast.10, s32[1,128]{1,0:T(1,128)} %bitcast.13, s32[1,192]{1,0:T(1,128)} %bitcast.12), custom_call_target="tpu_custom_call" | custom-call | flops 9663676416 | bytes 1572864 | tf_op jit(solution)/shard_map/pallas_call | solution.py:489
  72.6 0.0 copy-done.1
  72.6 0.0 copy-done.3
  72.7 0.0 copy-done.4
  72.7 0.3 conditional.1
  72.7 0.1 copy.10
  72.9 0.0 copy-start.2
  73.0 1.3 %copy.18 = f32[4096]{0:T(1024)} copy(f32[4096]{0:T(1024)} %get-tuple-element.48) | data formatting | bytes 32768
  74.3 0.0 copy-done.2
Async XLA Ops:
  7.2 65.5 %copy-start.1 = (f32[4096]{0:T(1024)S(1)}, f32[4096]{0:T(1024)}, u32[]{:S(2)}) copy-start(f32[4096]{0:T(1024)} %param.7) | copy-start | bytes 49156
  7.2 65.5 %copy-start.3 = (s32[192]{0:T(256)S(1)}, s32[192]{0:T(256)}, u32[]{:S(2)}) copy-start(s32[192]{0:T(256)} %param.9) | copy-start | bytes 2308
  7.2 65.5 %copy-start.4 = (s32[128]{0:T(128)S(1)}, s32[128]{0:T(128)}, u32[]{:S(2)}) copy-start(s32[128]{0:T(128)} %param.8) | copy-start | bytes 1540
  72.9 1.3 %copy-start.2 = (f32[192]{0:T(256)}, f32[192]{0:T(256)S(1)}, u32[]{:S(2)}) copy-start(f32[192]{0:T(256)S(1)} %get-tuple-element.49) | copy-start | bytes 2308

commit v4 on v3

--- a/solution.py
+++ b/solution.py
@@ -87,12 +87,24 @@
 
     barrier = pltpu.get_barrier_semaphore()
 
-    def greet(i, carry):
-        dev = lax.rem(me + i, ND)
-        pl.semaphore_signal(barrier, inc=1, device_id=(lax.rem(dev, R), lax.div(dev, R)), device_id_type=MESH)
-        return carry
-
-    lax.fori_loop(1, ND, greet, 0)
+    def others(act):
+        def wrap(value, size):
+            return jnp.where(value >= size, value - size, value)
+
+        for dr in range(1, R):
+            act(wrap(r + dr, R), c)
+
+        def column(dc, carry):
+            col = wrap(c + dc, C)
+            for dr in range(R):
+                act(wrap(r + dr, R), col)
+            return carry
+
+        lax.fori_loop(1, C, column, 0)
+
+    others(
+        lambda row, col: pl.semaphore_signal(barrier, inc=1, device_id=(row, col), device_id_type=MESH)
+    )
     idx[r] = jnp.full(idx.shape[1:], -1, jnp.int32)
     idx[r, :, 0:ns] = sel[...]
     idx[r, :, ns : ns + nk] = cand[...]
@@ -173,9 +185,11 @@
     start, packed = place(owner_cand, local[:, ns:], start, packed)
     packed = jnp.sum(packed, axis=1, keepdims=True)
     point = lax.broadcasted_iota(jnp.int32, (cap, rows), 1).astype(jnp.float32)
-    pick = jnp.where(point == packed - 1.0, 1.0, 0.0)
+    pick = jnp.where(point == packed - 1.0, 1.0, 0.0).astype(jnp.bfloat16)
     own = a * C + c
-    rows_owned = jnp.dot(pick, slab[...], precision=lax.Precision.HIGHEST, preferred_element_type=jnp.float32)
+    rows_owned = jnp.dot(pick, ph[m], preferred_element_type=jnp.float32) + jnp.dot(
+        pick, plo[m], preferred_element_type=jnp.float32
+    )
     qs[own, 0:sent] = rows_owned[0:sent]
 
     def q_copy(b, ssem, row, col):
@@ -286,16 +300,19 @@
     def arrive(b):
         q_copy(b, ql_send, r, c).wait_recv()
 
+    last = jnp.where(2 * c < C, C - 1, 0)
+    first = jnp.where(2 * c < C, 0, 1)
+
     def across_blocks(s):
         for i in range(1, A):
             other = lax.rem(a + i, A) * C + c
 
-            @pl.when(c - s >= 0)
+            @pl.when((c - s >= 0) & (c - s != last))
             def _():
                 arrive(other - s)
                 near_scores(other - s)
 
-            @pl.when((s > 0) & (c + s < C))
+            @pl.when((s > 0) & (c + s < C) & (c + s != last))
             def _():
                 arrive(other + s)
                 near_scores(other + s)
@@ -367,10 +384,21 @@
         other = lax.rem(a + i, A) * C
 
         def far_across(t, carry):
-            score(other, C, 2 * (1 - x) + lax.div(t, parts), lax.rem(t, parts))
+            score(other + first, C - 1, 2 * (1 - x) + lax.div(t, parts), lax.rem(t, parts))
             return carry
 
         lax.fori_loop(0, 2 * parts, far_across, 0)
+
+    for i in range(1, A):
+        other = lax.rem(a + i, A) * C
+        arrive(other + last)
+        split_block(other + last)
+
+        def last_scores(t, carry):
+            score(other + last, 1, lax.div(t, parts), lax.rem(t, parts))
+            return carry
+
+        lax.fori_loop(0, QUAD * parts, last_scores, 0)
 
     mx[m] = jnp.max(best[...], axis=0, keepdims=True)
 
@@ -401,28 +429,17 @@
 
     lax.fori_loop(0, NB, gains, 0)
 
-    def g_copy(slot, dev):
-        return remote(
-            gr.at[slot], gr.at[slot], g_send.at[dev], g_recv.at[slot], lax.rem(dev, R), lax.div(dev, R)
-        )
-
-    def g_start(i, carry):
-        g_copy(mine, lax.rem(me + i, ND)).start()
-        return carry
-
-    lax.fori_loop(1, ND, g_start, 0)
+    def g_copy(part, row, col):
+        return remote(part, part, g_send.at[0], g_recv.at[0], row, col)
+
+    others(lambda row, col: g_copy(gr.at[mine], row, col).start())
 
     for i in range(1, A):
         c_copy(lax.rem(a + i, A), lax.rem(a + i, A)).wait_recv()
     cov_out[...] = cov[...]
 
-    def g_wait(i, carry):
-        dev = lax.rem(me + i, ND)
-        row, col = lax.rem(dev, R), lax.div(dev, R)
-        g_copy(lax.rem(row, QUAD) * NB + lax.div(row, QUAD) * C + col, dev).wait_recv()
-        return carry
-
-    lax.fori_loop(1, ND, g_wait, 0)
+    every = g_copy(gr.at[pl.ds(0, ND - 1)], r, c)
+    every.wait_recv()
     totals = jnp.concatenate(
         [jnp.sum(gr[i * NB : (i + 1) * NB], axis=0) for i in range(QUAD)], axis=0
     )
@@ -466,11 +483,7 @@
     for i in range(1, A):
         c_copy(a, lax.rem(a + i, A)).wait_send()
 
-    def g_left(i, carry):
-        g_copy(mine, lax.rem(me + i, ND)).wait_send()
-        return carry
-
-    lax.fori_loop(1, ND, g_left, 0)
+    every.wait_send()
 
 
 def fused(R, C, slab_embed, coverage_old, sel_index, cand_index):
@@ -512,7 +525,7 @@
             dma((R,)), dma((R,)), dma((1,)), dma((1,)),
             dma((parts,)), dma((parts,)), dma((parts,)), dma((parts,)),
             dma((NB,)), dma((NB,)), dma((NB,)), dma((A - 1, NB)),
-            dma((QUAD,)), dma((QUAD,)), dma((A,)), dma((A,)), dma((ND,)), dma((ND,)),
+            dma((QUAD,)), dma((QUAD,)), dma((A,)), dma((A,)), dma((1,)), dma((1,)),
         ],
         compiler_params=pltpu.CompilerParams(
             collective_id=0, has_side_effects=True, vmem_limit_bytes=58 * 1024 * 1024

time: 81.3 us -> 80.1 us (0.985)
  Pallas kernels: 64.8 us -> 63.5 us
    pallas_call x1, Pallas kernels: 64.8 us -> 63.5 us  [fused(): pl.pallas_call(functools.partial(kernel, R, C, cap, sent), out_shape=(jax...]
where the time goes in v4:
time: 80.1 us; the launch traced here: 79.8 us
  Pallas kernels  63.5 us (79%)
  between operations  14.7 us (18%)
  local copies, waits for them, and re-layouts  1.42 us (2%)
    pallas_call x1, Pallas kernels, fused(): pl.pallas_call(functools.partial(kernel, R, C, cap, sent), out_shape=(jax...  63.5 us

profile of v4, /device:TPU:0, one launch (start us, length us, event | category | flops | bytes accessed | tf_op | source)
XLA Modules:
  0.0 79.8 jit_solution(9789665205129446703)
XLA Ops:
  7.2 0.0 copy-start.1
  7.2 0.0 copy-start.3
  7.2 0.0 copy-start.4
  7.2 63.5 %shard_map.63 = (f32[2,1,2048]{2,1,0:T(1,128)}, f32[192,1]{1,0:T(8,128)S(1)}, f32[1,1]{1,0:T(1,128)}) custom-call(f32[512,768]{1,0:T(8,128)} %slab.1, f32[2,1,2048]{2,1,0:T(1,128)} %bitcast.10, s32[1,128]{1,0:T(1,128)} %bitcast.13, s32[1,192]{1,0:T(1,128)} %bitcast.12), custom_call_target="tpu_custom_call" | custom-call | flops 9663676416 | bytes 1572864 | tf_op jit(solution)/shard_map/pallas_call | solution.py:502
  71.3 0.0 copy-done.1
  71.3 0.0 copy-done.3
  71.3 0.0 copy-done.4
  71.4 0.3 conditional.1
  71.4 0.1 copy.10
  71.6 0.0 copy-start.2
  71.6 1.3 %copy.18 = f32[4096]{0:T(1024)} copy(f32[4096]{0:T(1024)} %get-tuple-element.48) | data formatting | bytes 32768
  73.0 0.0 copy-done.2
Async XLA Ops:
  7.2 64.2 %copy-start.1 = (f32[4096]{0:T(1024)S(1)}, f32[4096]{0:T(1024)}, u32[]{:S(2)}) copy-start(f32[4096]{0:T(1024)} %param.7) | copy-start | bytes 49156
  7.2 64.2 %copy-start.3 = (s32[192]{0:T(256)S(1)}, s32[192]{0:T(256)}, u32[]{:S(2)}) copy-start(s32[192]{0:T(256)} %param.9) | copy-start | bytes 2308
  7.2 64.2 %copy-start.4 = (s32[128]{0:T(128)S(1)}, s32[128]{0:T(128)}, u32[]{:S(2)}) copy-start(s32[128]{0:T(128)} %param.8) | copy-start | bytes 1540
  71.6 1.3 %copy-start.2 = (f32[192]{0:T(256)}, f32[192]{0:T(256)S(1)}, u32[]{:S(2)}) copy-start(f32[192]{0:T(256)S(1)} %get-tuple-element.49) | copy-start | bytes 2308

commit v5 on v4

--- a/solution.py
+++ b/solution.py
@@ -46,6 +46,10 @@
 def halves(value):
     high = value.astype(jnp.bfloat16)
     return high, (value - high.astype(jnp.float32)).astype(jnp.bfloat16)
+
+
+def dot(left, right):
+    return jnp.dot(left, right, preferred_element_type=jnp.float32)
 
 
 def dot_nt(left, right):
@@ -140,9 +144,9 @@
 
     def split_part(source, slot, s):
         part = pl.ds(s * width, width)
-        high, low = halves(source[part])
-        ph[slot, part] = high
-        plo[slot, part] = low
+        high, low = halves(source[part].T)
+        ph[slot, s] = high
+        plo[slot, s] = low
 
     def split_points(source, slot):
         for s in range(parts):
@@ -187,9 +191,10 @@
     point = lax.broadcasted_iota(jnp.int32, (cap, rows), 1).astype(jnp.float32)
     pick = jnp.where(point == packed - 1.0, 1.0, 0.0).astype(jnp.bfloat16)
     own = a * C + c
-    rows_owned = jnp.dot(pick, ph[m], preferred_element_type=jnp.float32) + jnp.dot(
-        pick, plo[m], preferred_element_type=jnp.float32
-    )
+    rows_owned = jnp.zeros((cap, qs.shape[2]), jnp.float32)
+    for s in range(parts):
+        chosen = pick[:, s * width : (s + 1) * width]
+        rows_owned = rows_owned + (dot_nt(chosen, ph[m, s]) + dot_nt(chosen, plo[m, s]))
     qs[own, 0:sent] = rows_owned[0:sent]
 
     def q_copy(b, ssem, row, col):
@@ -225,13 +230,12 @@
         ql[pl.ds(b * cap, cap)] = low
 
     def score(first, count, slot, s):
-        part = pl.ds(s * width, width)
         out = pl.ds(slot * rows + s * width, width)
         block = pl.ds(first * cap, count * cap)
-        high, low = ph[slot, part], plo[slot, part]
+        high, low = ph[slot, s], plo[slot, s]
         n = count * cap
-        both = dot_nt(jnp.concatenate([qh[block], ql[block]], axis=0), high)
-        value = both[0:n] + both[n:] + dot_nt(qh[block], low)
+        both = dot(jnp.concatenate([qh[block], ql[block]], axis=0), high)
+        value = both[0:n] + both[n:] + dot(qh[block], low)
         sc[block, out] = value
         shift_by = bias[block]
         top = jnp.concatenate(
@@ -510,8 +514,8 @@
         out_specs=(vmem, vmem, vmem),
         scratch_shapes=[
             pltpu.VMEM((QUAD, rows, depth), f32),
-            pltpu.VMEM((QUAD, rows, depth), bf16),
-            pltpu.VMEM((QUAD, rows, depth), bf16),
+            pltpu.VMEM((QUAD, parts, depth, 256), bf16),
+            pltpu.VMEM((QUAD, parts, depth, 256), bf16),
             pltpu.VMEM((NB, cap, depth), f32),
             pltpu.VMEM((NB * cap, depth), bf16),
             pltpu.VMEM((NB * cap, depth), bf16),

time: 80.1 us -> 80 us (level)
  no operation moved by 1% of the time
where the time goes in v5:
time: 80 us; the launch traced here: 79.7 us
  Pallas kernels  63.4 us (79%)
  between operations  14.7 us (18%)
  local copies, waits for them, and re-layouts  1.42 us (2%)
    pallas_call x1, Pallas kernels, fused(): pl.pallas_call(functools.partial(kernel, R, C, cap, sent), out_shape=(jax...  63.4 us

profile of v5, /device:TPU:0, one launch (start us, length us, event | category | flops | bytes accessed | tf_op | source)
XLA Modules:
  0.0 79.7 jit_solution(5192743179229235716)
XLA Ops:
  7.2 0.0 copy-start.1
  7.2 0.0 copy-start.3
  7.2 0.0 copy-start.4
  7.2 63.4 %shard_map.63 = (f32[2,1,2048]{2,1,0:T(1,128)}, f32[192,1]{1,0:T(8,128)S(1)}, f32[1,1]{1,0:T(1,128)}) custom-call(f32[512,768]{1,0:T(8,128)} %slab.1, f32[2,1,2048]{2,1,0:T(1,128)} %bitcast.10, s32[1,128]{1,0:T(1,128)} %bitcast.13, s32[1,192]{1,0:T(1,128)} %bitcast.12), custom_call_target="tpu_custom_call" | custom-call | flops 9663676416 | bytes 1572864 | tf_op jit(solution)/shard_map/pallas_call | solution.py:506
  71.2 0.0 copy-done.1
  71.2 0.0 copy-done.3
  71.3 0.0 copy-done.4
  71.3 0.3 conditional.1
  71.3 0.1 copy.10
  71.5 0.0 copy-start.2
  71.6 1.3 %copy.18 = f32[4096]{0:T(1024)} copy(f32[4096]{0:T(1024)} %get-tuple-element.48) | data formatting | bytes 32768
  72.9 0.0 copy-done.2
Async XLA Ops:
  7.2 64.1 %copy-start.1 = (f32[4096]{0:T(1024)S(1)}, f32[4096]{0:T(1024)}, u32[]{:S(2)}) copy-start(f32[4096]{0:T(1024)} %param.7) | copy-start | bytes 49156
  7.2 64.1 %copy-start.3 = (s32[192]{0:T(256)S(1)}, s32[192]{0:T(256)}, u32[]{:S(2)}) copy-start(s32[192]{0:T(256)} %param.9) | copy-start | bytes 2308
  7.2 64.1 %copy-start.4 = (s32[128]{0:T(128)S(1)}, s32[128]{0:T(128)}, u32[]{:S(2)}) copy-start(s32[128]{0:T(128)} %param.8) | copy-start | bytes 1540
  71.5 1.3 %copy-start.2 = (f32[192]{0:T(256)}, f32[192]{0:T(256)S(1)}, u32[]{:S(2)}) copy-start(f32[192]{0:T(256)S(1)} %get-tuple-element.49) | copy-start | bytes 2308

commit v6 on v5

--- a/solution.py
+++ b/solution.py
@@ -61,7 +61,7 @@
     cov_out, gain_out, flag_out,
     pts, ph, plo, qs, qh, ql, sc, idx, bias, best, mx, cov, gr,
     idx_send, idx_recv, core_send, core_recv, x_send, x_recv, f_send, f_recv,
-    q_recv, ql_send, qr_send, qa_send, m_send, m_recv, c_send, c_recv, g_send, g_recv,
+    q_recv, ql_send, qr_send, qa_send, t_send, t_recv, m_send, m_recv, c_send, c_recv, g_send, g_recv,
 ):
     A = R // QUAD
     NB = A * C
@@ -123,12 +123,14 @@
     core_copy = remote(slab, pts.at[m], core_send.at[0], core_recv.at[0], base + m_core, c)
     core_copy.start()
 
+    half = width // 2
+
     def x_copy(s):
-        part = pl.ds(s * width, width)
+        part = pl.ds(s * half, half)
         return remote(slab.at[part], pts.at[m, part], x_send.at[s], x_recv.at[s], base + m_x, c)
 
     def x_landed(s):
-        part = pl.ds(s * width, width)
+        part = pl.ds(s * half, half)
         return remote(slab.at[part], pts.at[m_x, part], x_send.at[s], x_recv.at[s], base + m_x, c)
 
     def f_copy(s):
@@ -197,30 +199,52 @@
         rows_owned = rows_owned + (dot_nt(chosen, ph[m, s]) + dot_nt(chosen, plo[m, s]))
     qs[own, 0:sent] = rows_owned[0:sent]
 
-    def q_copy(b, ssem, row, col):
-        part = qs.at[b, pl.ds(0, sent)]
+    last = jnp.where(2 * c < C, C - 1, 0)
+    first = jnp.where(2 * c < C, 0, 1)
+    inward = jnp.where(2 * c < C, 1, -1)
+    head = -(-sent // 16) * 8
+
+    def q_copy(b, ssem, row, col, start=0, size=sent):
+        part = qs.at[b, pl.ds(start, size)]
         return remote(part, part, ssem.at[b], q_recv.at[b], row, col)
 
-    def q_right(b):
-        return q_copy(b, qr_send, r, c + 1)
-
-    def q_left(b):
-        return q_copy(b, ql_send, r, c - 1)
-
-    def q_across(b, i):
-        return q_copy(b, qa_send.at[i - 1], (lax.rem(a + i, A)) * QUAD + m, c)
+    def q_along(b, ssem, col):
+        return q_copy(b, ssem, r, col)
+
+    def q_across(b, i, size=sent):
+        return q_copy(b, qa_send.at[i - 1], lax.rem(a + i, A) * QUAD + m, c, 0, size)
+
+    def q_tail(i, col):
+        part = qs.at[lax.rem(a + i, A) * C + last, pl.ds(head, sent - head)]
+        return remote(part, part, t_send.at[i - 1, 0], t_recv.at[i - 1], r, col)
+
+    def q_edge(i, edge, col):
+        part = qs.at[lax.rem(a + i, A) * C + edge, pl.ds(head, sent - head)]
+        return remote(part, part, t_send.at[i - 1, 1], t_recv.at[i - 1], r, col)
+
+    def each_across(b, act):
+        whole = b != a * C + last
+
+        @pl.when(whole)
+        def _():
+            for i in range(1, A):
+                act(q_across(b, i))
+
+        @pl.when(jnp.logical_not(whole))
+        def _():
+            for i in range(1, A):
+                act(q_across(b, i, head))
 
     def spread(b):
-        for i in range(1, A):
-            q_across(b, i).start()
+        each_across(b, lambda copy: copy.start())
 
     @pl.when(c + 1 < C)
     def _():
-        q_right(own).start()
+        q_along(own, qr_send, c + 1).start()
 
     @pl.when(c > 0)
     def _():
-        q_left(own).start()
+        q_along(own, ql_send, c - 1).start()
 
     spread(own)
 
@@ -304,61 +328,79 @@
     def arrive(b):
         q_copy(b, ql_send, r, c).wait_recv()
 
-    last = jnp.where(2 * c < C, C - 1, 0)
-    first = jnp.where(2 * c < C, 0, 1)
+    inner = (c == C // 2) | (c == C // 2 - 1)
+
+    def inside(col):
+        return (col >= 0) & (col < C)
+
+    def across_block(i, s, side):
+        other = lax.rem(a + i, A) * C
+        col = c + side * s
+
+        @pl.when(inside(col) & (col != last))
+        def _():
+            arrive(other + col)
+
+            @pl.when(inner & (s == C // 2 - 1) & (side != inward))
+            def _():
+                q_edge(i, C - 1 - last, c + inward).start()
+
+            near_scores(other + col)
 
     def across_blocks(s):
         for i in range(1, A):
-            other = lax.rem(a + i, A) * C + c
-
-            @pl.when((c - s >= 0) & (c - s != last))
+            across_block(i, s, -inward)
+
+        @pl.when((s == C // 2 - 1) & (c > 0) & (c < C - 1))
+        def _():
+            for i in range(1, A):
+                q_tail(i, c).wait_recv()
+                q_tail(i, c - inward).start()
+
+        @pl.when(s > 0)
+        def _():
+            for i in range(1, A):
+                across_block(i, s, inward)
+
+    def hand_on(s, side):
+        @pl.when((s < C) & inside(c + side * s))
+        def _():
+            b = own + side * s
+            arrive(b)
+
+            @pl.when(inside(c - side))
             def _():
-                arrive(other - s)
-                near_scores(other - s)
-
-            @pl.when((s > 0) & (c + s < C) & (c + s != last))
+                q_along(b, ql_send, c - side).start()
+
+            spread(b)
+
+    def round_(s, carry):
+        hand_on(s, -inward)
+        hand_on(s, inward)
+
+        def scores(k, carry):
+            side = 2 * k - 1
+
+            @pl.when((s < C) & inside(c + side * s))
             def _():
-                arrive(other + s)
-                near_scores(other + s)
-
-    def round_(s, carry):
-        has_left = (s < C) & (c - s >= 0)
-        has_right = (s < C) & (c + s < C)
-
-        @pl.when(has_left)
-        def _():
-            b = own - s
-            arrive(b)
-
-            @pl.when(c + 1 < C)
-            def _():
-                q_right(b).start()
-
-            spread(b)
-
-        @pl.when(has_right)
-        def _():
-            b = own + s
-            arrive(b)
-
-            @pl.when(c > 0)
-            def _():
-                q_left(b).start()
-
-            spread(b)
-
-        @pl.when(has_left)
-        def _():
-            near_scores(own - s)
-
-        @pl.when(has_right)
-        def _():
-            near_scores(own + s)
-
-        @pl.when(s == C - 1)
+                near_scores(own + side * s)
+
+            return carry
+
+        lax.fori_loop(0, 2, scores, 0)
+
+        @pl.when(s == 2)
         def _():
             for t in range(parts):
                 x_landed(t).wait_recv()
+            for t in range(parts // 2):
+                f_copy(t).start()
+
+        @pl.when(s == C - 1)
+        def _():
+            for t in range(parts, 2 * parts):
+                x_landed(t).wait_recv()
+            for t in range(parts // 2, parts):
                 f_copy(t).start()
 
             def step(t, carry):
@@ -381,6 +423,13 @@
             lax.fori_loop(0, parts, step, 0)
 
         across_blocks(s - 1)
+
+        @pl.when(s == 1)
+        def _():
+            for t in range(parts):
+                x_copy(t).wait_send()
+                x_copy(parts + t).start()
+
         return carry
 
     lax.fori_loop(1, C + 1, round_, 0)
@@ -395,7 +444,12 @@
 
     for i in range(1, A):
         other = lax.rem(a + i, A) * C
-        arrive(other + last)
+        q_copy(other + last, ql_send, r, c, 0, head).wait_recv()
+
+        @pl.when((c == 0) | (c == C - 1))
+        def _():
+            q_tail(i, c).wait_recv()
+
         split_block(other + last)
 
         def last_scores(t, carry):
@@ -455,33 +509,45 @@
     core_copy.wait_send()
 
     for s in range(parts):
-        x_copy(s).wait_send()
+        x_copy(parts + s).wait_send()
         f_copy(s).wait_send()
 
+    @pl.when(c + 1 < C)
+    def _():
+        q_along(own, qr_send, c + 1).wait_send()
+
+    @pl.when(c > 0)
+    def _():
+        q_along(own, ql_send, c - 1).wait_send()
+
+    each_across(own, lambda copy: copy.wait_send())
+
+    @pl.when((c > 0) & (c < C - 1))
+    def _():
+        for i in range(1, A):
+            q_tail(i, c - inward).wait_send()
+
+    @pl.when(inner)
+    def _():
+        for i in range(1, A):
+            q_edge(i, C - 1 - last, c + inward).wait_send()
+
     def left(s, carry):
-        @pl.when(c - s >= 0)
-        def _():
-            @pl.when(c + 1 < C)
+        for side in (-1, 1):
+
+            @pl.when(inside(c + side * s))
             def _():
-                q_right(own - s).wait_send()
-
-            for i in range(1, A):
-                q_across(own - s, i).wait_send()
-
-        @pl.when(c + s < C)
-        def _():
-            @pl.when(c > 0)
-            def _():
-                q_left(own + s).wait_send()
-
-            @pl.when(s > 0)
-            def _():
-                for i in range(1, A):
-                    q_across(own + s, i).wait_send()
+                b = own + side * s
+
+                @pl.when(inside(c - side))
+                def _():
+                    q_along(b, ql_send, c - side).wait_send()
+
+                each_across(b, lambda copy: copy.wait_send())
 
         return carry
 
-    lax.fori_loop(0, C, left, 0)
+    lax.fori_loop(1, C, left, 0)
     for i in range(1, QUAD):
         m_copy(m, lax.rem(m + i, QUAD)).wait_send()
     for i in range(1, A):
@@ -527,8 +593,9 @@
             pltpu.VMEM((A, 1, span), f32),
             pltpu.VMEM((ND, NB, cap), f32),
             dma((R,)), dma((R,)), dma((1,)), dma((1,)),
-            dma((parts,)), dma((parts,)), dma((parts,)), dma((parts,)),
+            dma((2 * parts,)), dma((2 * parts,)), dma((parts,)), dma((parts,)),
             dma((NB,)), dma((NB,)), dma((NB,)), dma((A - 1, NB)),
+            dma((A - 1, 2)), dma((A - 1,)),
             dma((QUAD,)), dma((QUAD,)), dma((A,)), dma((A,)), dma((1,)), dma((1,)),
         ],
         compiler_params=pltpu.CompilerParams(

time: 80 us -> 81.7 us (1.021)
  Pallas kernels: 63.4 us -> 65.1 us
    pallas_call x1, Pallas kernels: 63.4 us -> 65.1 us  [fused(): pl.pallas_call(functools.partial(kernel, R, C, cap, sent), out_shape=(jax...]
where the time goes in v6:
time: 81.7 us; the launch traced here: 81.4 us
  Pallas kernels  65.1 us (80%)
  between operations  14.7 us (18%)
  local copies, waits for them, and re-layouts  1.42 us (2%)
    pallas_call x1, Pallas kernels, fused(): pl.pallas_call(functools.partial(kernel, R, C, cap, sent), out_shape=(jax...  65.1 us

profile of v6, /device:TPU:0, one launch (start us, length us, event | category | flops | bytes accessed | tf_op | source)
XLA Modules:
  0.0 81.4 jit_solution(5202379016792428992)
XLA Ops:
  7.2 0.0 copy-start.1
  7.2 0.0 copy-start.3
  7.2 0.0 copy-start.4
  7.2 65.1 %shard_map.63 = (f32[2,1,2048]{2,1,0:T(1,128)}, f32[192,1]{1,0:T(8,128)S(1)}, f32[1,1]{1,0:T(1,128)}) custom-call(f32[512,768]{1,0:T(8,128)} %slab.1, f32[2,1,2048]{2,1,0:T(1,128)} %bitcast.10, s32[1,128]{1,0:T(1,128)} %bitcast.13, s32[1,192]{1,0:T(1,128)} %bitcast.12), custom_call_target="tpu_custom_call" | custom-call | flops 9663676416 | bytes 1572864 | tf_op jit(solution)/shard_map/pallas_call | solution.py:572
  72.9 0.0 copy-done.1
  72.9 0.0 copy-done.3
  72.9 0.0 copy-done.4
  73.0 0.3 conditional.1
  73.0 0.1 copy.10
  73.2 0.0 copy-start.2
  73.2 1.3 %copy.18 = f32[4096]{0:T(1024)} copy(f32[4096]{0:T(1024)} %get-tuple-element.48) | data formatting | bytes 32768
  74.6 0.0 copy-done.2
Async XLA Ops:
  7.2 65.8 %copy-start.1 = (f32[4096]{0:T(1024)S(1)}, f32[4096]{0:T(1024)}, u32[]{:S(2)}) copy-start(f32[4096]{0:T(1024)} %param.7) | copy-start | bytes 49156
  7.2 65.8 %copy-start.3 = (s32[192]{0:T(256)S(1)}, s32[192]{0:T(256)}, u32[]{:S(2)}) copy-start(s32[192]{0:T(256)} %param.9) | copy-start | bytes 2308
  7.2 65.8 %copy-start.4 = (s32[128]{0:T(128)S(1)}, s32[128]{0:T(128)}, u32[]{:S(2)}) copy-start(s32[128]{0:T(128)} %param.8) | copy-start | bytes 1540
  73.2 1.3 %copy-start.2 = (f32[192]{0:T(256)}, f32[192]{0:T(256)S(1)}, u32[]{:S(2)}) copy-start(f32[192]{0:T(256)S(1)} %get-tuple-element.49) | copy-start | bytes 2308

commit v7 on v6

--- a/solution.py
+++ b/solution.py
@@ -141,7 +141,7 @@
         part = pl.ds(s * width, width)
         return remote(pts.at[m_diag, part], pts.at[m_diag, part], f_send.at[s], f_recv.at[s], base + m_core, c)
 
-    for s in range(parts):
+    for s in range(2 * parts):
         x_copy(s).start()
 
     def split_part(source, slot, s):
@@ -389,18 +389,11 @@
 
         lax.fori_loop(0, 2, scores, 0)
 
-        @pl.when(s == 2)
+        @pl.when(s == C - 1)
         def _():
             for t in range(parts):
-                x_landed(t).wait_recv()
-            for t in range(parts // 2):
-                f_copy(t).start()
-
-        @pl.when(s == C - 1)
-        def _():
-            for t in range(parts, 2 * parts):
-                x_landed(t).wait_recv()
-            for t in range(parts // 2, parts):
+                x_landed(2 * t).wait_recv()
+                x_landed(2 * t + 1).wait_recv()
                 f_copy(t).start()
 
             def step(t, carry):
@@ -423,12 +416,6 @@
             lax.fori_loop(0, parts, step, 0)
 
         across_blocks(s - 1)
-
-        @pl.when(s == 1)
-        def _():
-            for t in range(parts):
-                x_copy(t).wait_send()
-                x_copy(parts + t).start()
 
         return carry
 
@@ -509,7 +496,8 @@
     core_copy.wait_send()
 
     for s in range(parts):
-        x_copy(parts + s).wait_send()
+        x_copy(2 * s).wait_send()
+        x_copy(2 * s + 1).wait_send()
         f_copy(s).wait_send()
 
     @pl.when(c + 1 < C)

time: 81.7 us -> 81.1 us (level)
  no operation moved by 1% of the time
where the time goes in v7:
time: 81.1 us; the launch traced here: 80.9 us
  Pallas kernels  64.5 us (80%)
  between operations  14.7 us (18%)
  local copies, waits for them, and re-layouts  1.42 us (2%)
    pallas_call x1, Pallas kernels, fused(): pl.pallas_call(functools.partial(kernel, R, C, cap, sent), out_shape=(jax...  64.5 us

profile of v7, /device:TPU:0, one launch (start us, length us, event | category | flops | bytes accessed | tf_op | source)
XLA Modules:
  0.0 80.9 jit_solution(10420580498111326978)
XLA Ops:
  7.2 0.0 copy-start.1
  7.2 0.0 copy-start.3
  7.2 0.0 copy-start.4
  7.2 64.5 %shard_map.63 = (f32[2,1,2048]{2,1,0:T(1,128)}, f32[192,1]{1,0:T(8,128)S(1)}, f32[1,1]{1,0:T(1,128)}) custom-call(f32[512,768]{1,0:T(8,128)} %slab.1, f32[2,1,2048]{2,1,0:T(1,128)} %bitcast.10, s32[1,128]{1,0:T(1,128)} %bitcast.13, s32[1,192]{1,0:T(1,128)} %bitcast.12), custom_call_target="tpu_custom_call" | custom-call | flops 9663676416 | bytes 1572864 | tf_op jit(solution)/shard_map/pallas_call | solution.py:560
  72.4 0.0 copy-done.1
  72.4 0.0 copy-done.3
  72.4 0.0 copy-done.4
  72.4 0.3 conditional.1
  72.4 0.1 copy.10
  72.7 0.0 copy-start.2
  72.7 1.3 %copy.18 = f32[4096]{0:T(1024)} copy(f32[4096]{0:T(1024)} %get-tuple-element.48) | data formatting | bytes 32768
  74.0 0.0 copy-done.2
Async XLA Ops:
  7.2 65.2 %copy-start.1 = (f32[4096]{0:T(1024)S(1)}, f32[4096]{0:T(1024)}, u32[]{:S(2)}) copy-start(f32[4096]{0:T(1024)} %param.7) | copy-start | bytes 49156
  7.2 65.2 %copy-start.3 = (s32[192]{0:T(256)S(1)}, s32[192]{0:T(256)}, u32[]{:S(2)}) copy-start(s32[192]{0:T(256)} %param.9) | copy-start | bytes 2308
  7.2 65.2 %copy-start.4 = (s32[128]{0:T(128)S(1)}, s32[128]{0:T(128)}, u32[]{:S(2)}) copy-start(s32[128]{0:T(128)} %param.8) | copy-start | bytes 1540
  72.7 1.3 %copy-start.2 = (f32[192]{0:T(256)}, f32[192]{0:T(256)S(1)}, u32[]{:S(2)}) copy-start(f32[192]{0:T(256)S(1)} %get-tuple-element.49) | copy-start | bytes 2308
